TPU v7x, 128 devices: a whole 4x4x4 slice. The times are simulated.
128 devices in a mesh: seq: 32 (over x, y, core), exp: 4 (over z).
Axes of the slice: x: 4, y: 4, z: 4, core: 2. Of those that a mesh axis runs over, the one named last changes fastest.
Arguments:
- ssd_input: bfloat16 [16384, 8192], P('seq', 'exp'), may hold values from -26 to 26
- dt_raw: float32 [16384, 128], P('seq', 'exp'), may hold values from -4 to 4
- dt_bias: float32 [128], P('exp'), may hold values from -1 to 1
- log_decay: float32 [16384, 128], P('seq', 'exp'), may hold values from -2 to 0, as said below
- input_map: bfloat16 [16384, 8, 128], P('seq', 'exp'), may hold values from -5 to 5
- output_map: bfloat16 [16384, 8, 128], P('seq', 'exp'), may hold values from -0.5 to 0.5
- head_group: int32 [128], P('exp'), may hold values from 0 to 7
- d_skip: float32 [128], P('exp'), may hold values from 0.5 to 2
- norm_gain: float32 [8192], P('exp'), may hold values from 0.5 to 1.5
- w_out: bfloat16 [8192, 2048], P('exp'), may hold values from -0.0625 to 0.0625
- residual: bfloat16 [16384, 2048], P(('seq', 'exp')), may hold values from -26 to 26
- moe_gain: float32 [2048], replicated, may hold values from 0.5 to 1.5
- w_router: bfloat16 [2048, 64], replicated, may hold values from -0.125 to 0.125
- expert_ids: int32 [16384, 4], P(('seq', 'exp')), may hold values from 0 to 63, as said below
- w_gate: bfloat16 [128, 2048, 1024], P(('seq', 'exp')), may hold values from -0.125 to 0.125
- w_up: bfloat16 [128, 2048, 1024], P(('seq', 'exp')), may hold values from -0.125 to 0.125
- w_down: bfloat16 [128, 1024, 2048], P(('seq', 'exp')), may hold values from -0.125 to 0.125
Outputs:
- mixed: bfloat16 [16384, 2048], P(('seq', 'exp'))
Inputs may be any that keep to these rules, and one draw needn't show every extreme that they name: `log_decay`: every entry is negative. `expert_ids`: each row names 4 different experts. In each aligned block of 128 rows (the rows of one device) no expert is named by more than 14 rows, and one expert, the same in every block, is named by exactly 14 rows of every block.
All inputs are finite; a program needn't handle non-finite values.
Results may differ from a plain program's by a relative error of at most 0.009.
Values may be sent and summed in bfloat16 or wider, within the bound.
No kernel may reach another device: no remote copies, remote signals or barrier semaphores. Data moves between devices by JAX's collectives and lax.ppermute only.
A program may use at most 192 MiB of HBM per device.

v0:
```python
import functools

import jax
import jax.numpy as jnp
from jax import lax
from jax.experimental import pallas as pl
from jax.experimental.pallas import tpu as pltpu
from jax.sharding import PartitionSpec as P

P_SIZE = 64
NST = 128
G = 8
BLOCK = 256
PAIR = 2 * P_SIZE
STEP_PAIRS = 4
SLOTS = 14
CHUNKS = 2
ROW = 8
CELL = 256

EPS = 1e-06
F32 = jnp.float32
BF16 = jnp.bfloat16
MIB = 1024 * 1024


def dot(a, b):
    return jnp.dot(a, b, preferred_element_type=F32)


def lanes_of_first(shape):
    return lax.broadcasted_iota(jnp.int32, shape, 1) < P_SIZE


def columns_of(first_row, second_row):
    length = first_row.shape[1]
    rows = jnp.concatenate(
        [
            jnp.broadcast_to(first_row, (P_SIZE, length)),
            jnp.broadcast_to(second_row, (P_SIZE, length)),
        ],
        axis=0,
    )
    return rows.T


def lane_pair(first, second):
    return jnp.concatenate(
        [jnp.broadcast_to(first, (1, P_SIZE)), jnp.broadcast_to(second, (1, P_SIZE))], axis=1
    )


def split_pair(values):
    first = lanes_of_first(values.shape)
    zero = jnp.zeros_like(values)
    return jnp.concatenate([jnp.where(first, values, zero), jnp.where(first, zero, values)], axis=0)


def prep_kernel(raw_ref, bias_ref, decay_ref, out_ref):
    value = raw_ref[...] + bias_ref[...]
    size = jnp.maximum(value, 0.0) + jnp.log(1.0 + jnp.exp(-jnp.abs(value)))
    upto = jnp.where(
        lax.broadcasted_iota(jnp.int32, (BLOCK, BLOCK), 0)
        <= lax.broadcasted_iota(jnp.int32, (BLOCK, BLOCK), 1),
        1.0,
        0.0,
    ).astype(BF16)
    heads, length = size.shape
    for b in range(length // BLOCK):
        rows = slice(b * BLOCK, (b + 1) * BLOCK)
        rest = decay_ref[:, rows]
        terms = []
        for _ in range(3):
            terms.append(rest.astype(BF16))
            rest = rest - terms[-1].astype(F32)
        sums = dot(jnp.concatenate(terms, axis=0), upto)
        running = sums[:heads] + sums[heads : 2 * heads] + sums[2 * heads :]
        out_ref[0, :, rows] = running
        out_ref[1, :, rows] = size[:, rows]
        out_ref[2, :, rows] = jnp.exp(running[:, BLOCK - 1 :] - running) * size[:, rows]
        out_ref[3, :, rows] = jnp.exp(running)


def states_kernel(
    slot_ref,
    x_ref,
    prep_ref,
    m0,
    m1,
    m2,
    m3,
    fresh_hbm,
    send_hbm,
    maps,
    fresh_all,
    send_all,
    fresh_sem,
    send_sem,
):
    step = pl.program_id(0)
    steps = fresh_sem.shape[0]

    def out_copies(at):
        pairs = pl.ds(at * STEP_PAIRS, STEP_PAIRS)
        pieces = pl.ds(at * 2 * STEP_PAIRS, 2 * STEP_PAIRS)
        return [
            pltpu.make_async_copy(send_all.at[pieces], send_hbm.at[pieces], send_sem.at[at]),
            pltpu.make_async_copy(fresh_all.at[pairs], fresh_hbm.at[pairs], fresh_sem.at[at]),
        ]

    @pl.when(step == 0)
    def _():
        maps[0:2] = m0[...]
        maps[2:4] = m1[...]
        maps[4:6] = m2[...]
        maps[6:8] = m3[...]

    for p in range(STEP_PAIRS):
        slots = [slot_ref[step * 2 * STEP_PAIRS + 2 * p + i] for i in range(2)]
        x = x_ref[:, p * PAIR : (p + 1) * PAIR].astype(F32)
        weight = columns_of(prep_ref[2, 2 * p : 2 * p + 1, :], prep_ref[2, 2 * p + 1 : 2 * p + 2, :])
        scaled = (x * weight).astype(BF16)
        fresh = []
        for b in range(2):
            rows = slice(b * BLOCK, (b + 1) * BLOCK)
            both = split_pair(scaled[rows])
            left = jnp.concatenate([maps[slots[0], :, rows], maps[slots[1], :, rows]], axis=1)
            fresh.append(dot(left, both))
        ends = [
            lane_pair(
                prep_ref[3, 2 * p : 2 * p + 1, e - 1 : e],
                prep_ref[3, 2 * p + 1 : 2 * p + 2, e - 1 : e],
            )
            for e in (BLOCK, 2 * BLOCK)
        ]
        fresh_all[step * STEP_PAIRS + p] = fresh[0]
        final = (ends[1] * fresh[0] + fresh[1]).astype(BF16)
        decay = ends[0] * ends[1]
        high = decay.astype(BF16).astype(F32)
        row = lax.broadcasted_iota(jnp.int32, (8, PAIR), 0)
        tail = jnp.where(row == 0, high, jnp.where(row == 1, decay - high, 0.0)).astype(BF16)
        for i in range(2):
            piece = step * 2 * STEP_PAIRS + 2 * p + i
            send_all[piece, 0:64] = final[64 * i : 64 * (i + 1)]
            send_all[piece, 64:72] = tail
    for copy in out_copies(step):
        copy.start()

    @pl.when(step == steps - 1)
    def _():
        for at in range(steps):
            for copy in out_copies(at):
                copy.wait()


def scan_kernel(in_ref, out_ref):
    state = jnp.zeros((64, PAIR), F32)
    for j in range(in_ref.shape[0]):
        out_ref[j] = state.astype(BF16)
        tail = in_ref[j, 64:72].astype(F32)
        decay = tail[0:1] + tail[1:2]
        state = decay * state + in_ref[j, 0:64].astype(F32)


def within_kernel(
    slot_ref, x_ref, prep_ref, skip_ref, i0, i1, i2, i3, o0, o1, o2, o3, out_ref, scores
):
    step = pl.program_id(0)

    @pl.when(step == 0)
    def _():
        inputs = [ref.at[i] for ref in (i0, i1, i2, i3) for i in range(2)]
        outputs = [ref.at[i] for ref in (o0, o1, o2, o3) for i in range(2)]
        for g in range(G):
            for b in range(2):
                rows = slice(b * BLOCK, (b + 1) * BLOCK)
                scores[g, b] = dot(outputs[g][rows, :], inputs[g][:, rows])

    half = BLOCK // 2
    causal = lax.broadcasted_iota(jnp.int32, (half, half), 0) >= lax.broadcasted_iota(
        jnp.int32, (half, half), 1
    )
    for p in range(STEP_PAIRS):
        columns = slice(p * PAIR, (p + 1) * PAIR)
        slots = [slot_ref[step * 2 * STEP_PAIRS + 2 * p + i] for i in range(2)]
        for b in range(2):
            rows = slice(b * BLOCK, (b + 1) * BLOCK)
            x = x_ref[rows, columns]
            early, late = [], []
            for i in range(2):
                running = prep_ref[0, 2 * p + i : 2 * p + i + 1, rows]
                size = prep_ref[1, 2 * p + i : 2 * p + i + 1, rows]
                down = jnp.broadcast_to(running, (half, BLOCK)).T

                def tile(t, s, masked):
                    ts, ss = slice(t * half, (t + 1) * half), slice(s * half, (s + 1) * half)
                    spread = down[ts] - running[:, ss]
                    score = scores[slots[i], b, ts, ss]
                    value = score * jnp.exp(spread) * size[:, ss]
                    return (jnp.where(causal, value, 0.0) if masked else value).astype(BF16)

                early.append(tile(0, 0, True))
                late.append(tile(1, 0, False))
                late.append(tile(1, 1, True))
            both = split_pair(x)
            first = jnp.concatenate([both[0:half], both[BLOCK : BLOCK + half]], axis=0)
            skipped = skip_ref[:, columns] * x.astype(F32)
            top = dot(jnp.concatenate(early, axis=1), first)
            bottom = dot(jnp.concatenate(late, axis=1), both)
            out_ref[b * BLOCK : b * BLOCK + half, columns] = (top + skipped[0:half]).astype(BF16)
            out_ref[b * BLOCK + half : (b + 1) * BLOCK, columns] = (bottom + skipped[half:]).astype(
                BF16
            )


def project_kernel(
    slot_ref,
    place_ref,
    within_ref,
    prep_ref,
    gain_ref,
    enter_ref,
    fresh_ref,
    o0,
    o1,
    o2,
    o3,
    w_ref,
    own_ref,
    up_ref,
    far_ref,
    down_ref,
    maps,
    normed,
    total,
):
    step = pl.program_id(0)

    @pl.when(step == 0)
    def _():
        maps[0:2] = o0[...]
        maps[2:4] = o1[...]
        maps[4:6] = o2[...]
        maps[6:8] = o3[...]
        total[...] = jnp.zeros_like(total)

    same = (
        lax.broadcasted_iota(jnp.int32, (2 * PAIR, PAIR), 0) % PAIR // P_SIZE
        == lax.broadcasted_iota(jnp.int32, (2 * PAIR, PAIR), 1) // P_SIZE
    )
    summing = jnp.where(same, 1.0, 0.0).astype(BF16)
    for p in range(STEP_PAIRS):
        columns = slice(p * PAIR, (p + 1) * PAIR)
        slots = [slot_ref[step * 2 * STEP_PAIRS + 2 * p + i] for i in range(2)]
        growth = columns_of(prep_ref[3, 2 * p : 2 * p + 1, :], prep_ref[3, 2 * p + 1 : 2 * p + 2, :])
        first_end = lane_pair(
            prep_ref[3, 2 * p : 2 * p + 1, BLOCK - 1 : BLOCK], prep_ref[3, 2 * p + 1 : 2 * p + 2, BLOCK - 1 : BLOCK]
        )
        arriving = enter_ref[p].astype(F32)
        entering = [arriving, first_end * arriving + fresh_ref[p]]
        for b in range(2):
            rows = slice(b * BLOCK, (b + 1) * BLOCK)
            left = jnp.concatenate([maps[slots[0], rows, :], maps[slots[1], rows, :]], axis=1)
            carried = dot(left, split_pair(entering[b].astype(BF16)))
            y = within_ref[rows, columns].astype(F32) + carried * growth[rows]
            square = y * y
            high = square.astype(BF16)
            low = (square - high.astype(F32)).astype(BF16)
            mean = dot(jnp.concatenate([high, low], axis=1), summing) * (1.0 / P_SIZE)
            normed[rows, columns] = (y * lax.rsqrt(mean + EPS) * gain_ref[:, columns]).astype(BF16)
    total[...] += dot(normed[...], w_ref[...])

    @pl.when(step == pl.num_programs(0) - 1)
    def _():
        share = own_ref.shape[0]

        def rows_for(offset):
            place = lax.rem(place_ref[0] + offset, 4)
            rows = total[pl.ds(pl.multiple_of(place * share, share), share), :]
            return rows.astype(BF16)

        own_ref[...] = rows_for(0)
        up_ref[...] = rows_for(1)
        far_ref[...] = rows_for(2)
        down_ref[...] = rows_for(3)


def put_cells(stage, j, value):
    for h in range(2):
        stage[h, pl.ds(j, value.shape[0], stride=ROW), :] = value[:, h * 128 : (h + 1) * 128]


def take_cells(stage, j, count):
    return jnp.concatenate(
        [stage[h, pl.ds(j, count, stride=ROW), :] for h in range(2)], axis=1
    ).astype(BF16)


def fill_stage(stage, rows_ref):
    for h in range(2):
        stage[h] = rows_ref[:, h * 128 : (h + 1) * 128].astype(F32)


def drain_stage(stage, rows_ref):
    for h in range(2):
        rows_ref[:, h * 128 : (h + 1) * 128] = stage[h].astype(BF16)


def tokens_kernel(
    residual_ref,
    own_ref,
    prev_ref,
    far_ref,
    next_ref,
    gain_ref,
    router_ref,
    ids_ref,
    stream_ref,
    weight_ref,
    *rest,
    ring,
):
    out_refs, (stage, tokens) = rest[:-2], rest[-2:]
    share, width = stream_ref.shape
    stream = (
        residual_ref[...].astype(F32)
        + own_ref[...].astype(F32)
        + prev_ref[...].astype(F32)
        + far_ref[...].astype(F32)
        + next_ref[...].astype(F32)
    )
    stream_ref[...] = stream
    square = jnp.mean(stream * stream, axis=-1, keepdims=True)
    tokens[...] = (stream * lax.rsqrt(square + EPS) * gain_ref[...]).astype(BF16)
    experts = router_ref.shape[1]
    place = lax.broadcasted_iota(jnp.int32, (share, experts), 1)
    hosted = place % ring * (experts // ring) + place // ring
    routed = jnp.zeros((share, experts), F32)
    for k in range(ids_ref.shape[1]):
        routed = routed + jnp.where(ids_ref[:, k : k + 1] == hosted, 1.0, 0.0)
    earlier = jnp.where(
        lax.broadcasted_iota(jnp.int32, (share, share), 0)
        > lax.broadcasted_iota(jnp.int32, (share, share), 1),
        1.0,
        0.0,
    ).astype(BF16)
    rank = dot(earlier, routed.astype(BF16))
    key = jnp.where(routed > 0.5, rank, -1.0).astype(BF16)
    logits = dot(tokens[...], router_ref[...])
    weight = 1.0 / (1.0 + jnp.exp(-logits))
    high = weight.astype(BF16)
    low = (weight - high.astype(F32)).astype(BF16)
    chunk = SLOTS // CHUNKS
    rows = experts * chunk
    spread = jnp.where(
        lax.broadcasted_iota(jnp.int32, (experts, rows), 0)
        == lax.broadcasted_iota(jnp.int32, (experts, rows), 1) // chunk,
        1.0,
        0.0,
    ).astype(BF16)
    wide = dot(jnp.concatenate([key, high, low], axis=0), spread)
    ranks, highs, lows = wide[:share], wide[share : 2 * share], wide[2 * share :]
    slot = (lax.broadcasted_iota(jnp.int32, (share, rows), 1) % chunk).astype(F32)
    for i in range(CHUNKS):
        placed = ranks == slot + float(i * chunk)
        weight_ref[i, :share] = jnp.where(placed, highs, 0.0).astype(BF16)
        weight_ref[i, share:] = jnp.where(placed, lows, 0.0).astype(BF16)
        pick = jnp.where(placed, 1.0, 0.0).T.astype(BF16)
        for j in range(ROW):
            put_cells(stage, j, dot(pick, tokens[:, j * CELL : (j + 1) * CELL]))
        drain_stage(stage, out_refs[i])


def experts_kernel(
    x_ref,
    g0,
    u0,
    d0,
    g1,
    u1,
    d1,
    out_ref,
    stage,
    rows,
    hidden,
    wide,
    deep,
    wide_sem,
    deep_sem,
):
    count, width = rows.shape
    unit = g0.shape[1]
    n_wide, n_deep = wide.shape[0], deep.shape[0]
    wide_step, deep_step = 2 * unit // n_wide, width // n_deep
    halves = [(g0, u0, d0), (g1, u1, d1)]

    def copies(s):
        if s < n_wide:
            half = halves[s * wide_step // unit]
            columns = pl.ds(s * wide_step % unit, wide_step)
            return [
                pltpu.make_async_copy(half[i].at[:, columns], wide.at[s, i], wide_sem.at[s, i])
                for i in range(2)
            ]
        s -= n_wide
        columns = pl.ds(s * deep_step, deep_step)
        return [
            pltpu.make_async_copy(
                halves[i][2].at[:, columns], deep.at[s, pl.ds(i * unit, unit)], deep_sem.at[s, i]
            )
            for i in range(2)
        ]

    total_steps = n_wide + n_deep
    ahead = 3
    for s in range(ahead):
        for copy in copies(s):
            copy.start()
    fill_stage(stage, x_ref)
    for j in range(ROW):
        rows[:, j * CELL : (j + 1) * CELL] = take_cells(stage, j, count)
    for s in range(total_steps):
        if s + ahead < total_steps:
            for copy in copies(s + ahead):
                copy.start()
        for copy in copies(s):
            copy.wait()
        if s < n_wide:
            gated = dot(rows[...], wide[s, 0])
            raised = dot(rows[...], wide[s, 1])
            hidden[:, s * wide_step : (s + 1) * wide_step] = (
                gated / (1.0 + jnp.exp(-gated)) * raised
            ).astype(BF16)
        else:
            d = s - n_wide
            for c in range(deep_step // CELL):
                part = dot(hidden[...], deep[d, :, c * CELL : (c + 1) * CELL])
                put_cells(stage, d * (deep_step // CELL) + c, part)
    drain_stage(stage, out_ref)


def combine_kernel(base_ref, weight_ref, rows_ref, out_ref, stage):
    share = base_ref.shape[0]
    count = weight_ref.shape[1]
    fill_stage(stage, rows_ref)
    for j in range(ROW):
        columns = slice(j * CELL, (j + 1) * CELL)
        part = dot(weight_ref[...], take_cells(stage, j, count))
        out_ref[:, columns] = (base_ref[:, columns] + part[:share] + part[share:]).astype(
            out_ref.dtype
        )


def whole(shape):
    return pl.BlockSpec(shape, lambda s, *_: (0,) * len(shape))


def params(mib=60):
    return pltpu.CompilerParams(
        dimension_semantics=("arbitrary",), vmem_limit_bytes=mib * MIB
    )


def body(
    ssd_input,
    dt_raw,
    dt_bias,
    log_decay,
    input_map,
    output_map,
    head_group,
    d_skip,
    norm_gain,
    w_out,
    residual,
    moe_gain,
    w_router,
    expert_ids,
    w_gate,
    w_up,
    w_down,
):
    length = ssd_input.shape[0]
    heads = dt_raw.shape[1]
    width = w_out.shape[1]
    share = residual.shape[0]
    me = lax.axis_index("exp")
    ring = lax.axis_size("exp")
    seq_count = lax.axis_size("seq")
    nxt = [(i, (i + 1) % ring) for i in range(ring)]
    prv = [(i, (i - 1) % ring) for i in range(ring)]
    partner = [(i, i ^ 1) for i in range(seq_count)]
    steps = heads // (2 * STEP_PAIRS)
    columns = STEP_PAIRS * PAIR

    opposite = [(i, (i + 2) % ring) for i in range(ring)]

    def gather_maps(own):
        far = lax.ppermute(own, "exp", opposite)
        return own, lax.ppermute(own, "exp", prv), far, lax.ppermute(own, "exp", nxt)

    in_maps = gather_maps(input_map.transpose(1, 2, 0))
    out_maps = gather_maps(output_map.transpose(1, 0, 2))
    slot = (lax.rem(head_group // 2 - me + ring, ring) * 2 + head_group % 2).astype(jnp.int32)

    prep = pl.pallas_call(
        prep_kernel,
        out_shape=jax.ShapeDtypeStruct((4, heads, length), F32),
        compiler_params=pltpu.CompilerParams(vmem_limit_bytes=16 * MIB),
        cost_estimate=pl.CostEstimate(
            flops=30_000_000, bytes_accessed=400_000, transcendentals=100_000
        ),
        name="prep",
    )(dt_raw.T, dt_bias[:, None], log_decay.T)
    skip_lanes = jnp.repeat(d_skip, P_SIZE)[None, :]
    gain_lanes = norm_gain[None, :]

    x_spec = pl.BlockSpec((length, columns), lambda s, *_: (0, s))
    prep_spec = pl.BlockSpec((4, 2 * STEP_PAIRS, length), lambda s, *_: (0, s, 0))
    lane_spec = pl.BlockSpec((1, columns), lambda s, *_: (0, s))
    state_spec = pl.BlockSpec((STEP_PAIRS, NST, PAIR), lambda s, *_: (s, 0, 0))
    in_specs = [whole((2, NST, length))] * 4
    out_specs = [whole((2, length, NST))] * 4

    fresh, sending = pl.pallas_call(
        states_kernel,
        grid_spec=pltpu.PrefetchScalarGridSpec(
            num_scalar_prefetch=1,
            grid=(steps,),
            in_specs=[x_spec, prep_spec] + in_specs,
            out_specs=[pl.BlockSpec(memory_space=pltpu.HBM)] * 2,
            scratch_shapes=[
                pltpu.VMEM((G, NST, length), BF16),
                pltpu.VMEM((heads // 2, NST, PAIR), F32),
                pltpu.VMEM((heads, 72, PAIR), BF16),
                pltpu.SemaphoreType.DMA((steps,)),
                pltpu.SemaphoreType.DMA((steps,)),
            ],
        ),
        out_shape=[
            jax.ShapeDtypeStruct((heads // 2, NST, PAIR), F32),
            jax.ShapeDtypeStruct((heads, 72, PAIR), BF16),
        ],
        compiler_params=params(16),
        cost_estimate=pl.CostEstimate(
            flops=600_000_000, bytes_accessed=5_000_000, transcendentals=0
        ),
        name="states",
    )(slot, ssd_input, prep, *in_maps)

    sending, own_gate = lax.optimization_barrier((sending, w_gate[0]))
    other_gate = lax.ppermute(own_gate, "seq", partner)
    other_up = lax.ppermute(w_up[0], "seq", partner)
    other_down = lax.ppermute(w_down[0], "seq", partner)

    arrived = lax.all_to_all(sending, "seq", split_axis=0, concat_axis=0, tiled=True)
    prefix = pl.pallas_call(
        scan_kernel,
        out_shape=jax.ShapeDtypeStruct((seq_count, 64, PAIR), BF16),
        compiler_params=pltpu.CompilerParams(vmem_limit_bytes=16 * MIB),
        name="scan",
    )(arrived)
    entering = lax.all_to_all(prefix, "seq", split_axis=0, concat_axis=0, tiled=True)
    entering = entering.reshape(heads // 2, NST, PAIR)

    within = pl.pallas_call(
        within_kernel,
        grid_spec=pltpu.PrefetchScalarGridSpec(
            num_scalar_prefetch=1,
            grid=(steps,),
            in_specs=[x_spec, prep_spec, lane_spec] + in_specs + out_specs,
            out_specs=x_spec,
            scratch_shapes=[pltpu.VMEM((G, 2, BLOCK, BLOCK), F32)],
        ),
        out_shape=jax.ShapeDtypeStruct(ssd_input.shape, BF16),
        compiler_params=params(),
        cost_estimate=pl.CostEstimate(
            flops=12_000_000_000, bytes_accessed=8_000_000, transcendentals=4_000_000
        ),
        name="within",
    )(slot, ssd_input, prep, skip_lanes, *in_maps, *out_maps)

    vmem = pl.BlockSpec(memory_space=pltpu.VMEM)
    hbm = pl.BlockSpec(memory_space=pl.ANY)
    within, other_gate = lax.optimization_barrier((within, other_gate))
    own, up, far, down = pl.pallas_call(
        project_kernel,
        grid_spec=pltpu.PrefetchScalarGridSpec(
            num_scalar_prefetch=2,
            grid=(steps,),
            in_specs=[x_spec, prep_spec, lane_spec, state_spec, state_spec]
            + out_specs
            + [pl.BlockSpec((columns, width), lambda s, *_: (s, 0))],
            out_specs=[whole((share, width))] * 4,
            scratch_shapes=[
                pltpu.VMEM((G, length, NST), BF16),
                pltpu.VMEM((length, columns), BF16),
                pltpu.VMEM((length, width), F32),
            ],
        ),
        out_shape=[jax.ShapeDtypeStruct((share, width), BF16)] * 4,
        compiler_params=params(),
        cost_estimate=pl.CostEstimate(
            flops=6_000_000_000, bytes_accessed=16_000_000, transcendentals=0
        ),
        name="project",
    )(slot, me[None].astype(jnp.int32), within, prep, gain_lanes, entering, fresh, *out_maps, w_out)

    from_prev = lax.ppermute(up, "exp", nxt)
    from_far = lax.ppermute(far, "exp", opposite)
    from_next = lax.ppermute(down, "exp", prv)

    experts = w_router.shape[1]
    per_group = experts // ring
    router = w_router.reshape(-1, ring, per_group).swapaxes(1, 2).reshape(-1, experts)
    chunk = SLOTS // CHUNKS
    count = experts * chunk
    cells = (count * ROW, CELL)
    stage = (2, count * ROW, CELL // 2)
    stream, weights, *outgoing = pl.pallas_call(
        functools.partial(tokens_kernel, ring=ring),
        out_shape=[
            jax.ShapeDtypeStruct((share, width), F32),
            jax.ShapeDtypeStruct((CHUNKS, 2 * share, count), BF16),
        ]
        + [jax.ShapeDtypeStruct(cells, BF16)] * CHUNKS,
        scratch_shapes=[pltpu.VMEM(stage, F32), pltpu.VMEM((share, width), BF16)],
        compiler_params=pltpu.CompilerParams(vmem_limit_bytes=32 * MIB),
        cost_estimate=pl.CostEstimate(
            flops=1_000_000_000, bytes_accessed=8_000_000, transcendentals=0
        ),
        name="tokens",
    )(residual, own, from_prev, from_far, from_next, moe_gain[None, :], router, expert_ids)

    cores = [
        [(c // ring * 2 + h) * ring + c % ring for c in range(experts)] for h in range(2)
    ]

    def swap(rows):
        swapped = lax.all_to_all(
            rows.reshape(count, ROW, CELL),
            ("seq", "exp"),
            split_axis=0,
            concat_axis=0,
            tiled=True,
            axis_index_groups=cores,
        )
        return swapped.reshape(cells)

    unit = w_gate.shape[2]
    run_experts = pl.pallas_call(
        experts_kernel,
        in_specs=[vmem] + [hbm] * 6,
        out_specs=vmem,
        out_shape=jax.ShapeDtypeStruct(cells, BF16),
        scratch_shapes=[
            pltpu.VMEM(stage, F32),
            pltpu.VMEM((count, width), BF16),
            pltpu.VMEM((count, 2 * unit), BF16),
            pltpu.VMEM((8, 2, width, unit // 4), BF16),
            pltpu.VMEM((4, 2 * unit, width // 4), BF16),
            pltpu.SemaphoreType.DMA((8, 2)),
            pltpu.SemaphoreType.DMA((4, 2)),
        ],
        compiler_params=pltpu.CompilerParams(vmem_limit_bytes=60 * MIB),
        cost_estimate=pl.CostEstimate(
            flops=12 * count * width * unit,
            bytes_accessed=28_000_000,
            transcendentals=0,
        ),
        name="experts",
    )

    def combine(base, weight, rows, dtype):
        return pl.pallas_call(
            combine_kernel,
            out_shape=jax.ShapeDtypeStruct((share, width), dtype),
            scratch_shapes=[pltpu.VMEM(stage, F32)],
            compiler_params=pltpu.CompilerParams(vmem_limit_bytes=24 * MIB),
            cost_estimate=pl.CostEstimate(
                flops=500_000_000, bytes_accessed=4_000_000, transcendentals=0
            ),
            name="combine",
        )(base, weight, rows)

    arrivals = [swap(rows) for rows in outgoing]
    returned = [
        swap(
            run_experts(
                rows, w_gate[0], w_up[0], w_down[0], other_gate, other_up, other_down
            )
        )
        for rows in arrivals
    ]
    mixed = stream
    for i in range(CHUNKS):
        mixed = combine(mixed, weights[i], returned[i], BF16 if i == CHUNKS - 1 else F32)
    return mixed


def solution(mesh):
    return jax.shard_map(
        body,
        mesh=mesh,
        in_specs=(
            P("seq", "exp"),
            P("seq", "exp"),
            P("exp"),
            P("seq", "exp"),
            P("seq", "exp", None),
            P("seq", "exp", None),
            P("exp"),
            P("exp"),
            P("exp"),
            P("exp", None),
            P(("seq", "exp"), None),
            P(),
            P(),
            P(("seq", "exp"), None),
            P(("seq", "exp"), None, None),
            P(("seq", "exp"), None, None),
            P(("seq", "exp"), None, None),
        ),
        out_specs=P(("seq", "exp"), None),
        check_vma=False,
    )
```

profile of v0, /device:TPU:0, one launch (start us, length us, event | category | flops | bytes accessed | tf_op | source)
XLA Modules:
  0.0 250.6 jit_solution(10205283331006090604)
XLA Ops:
  1.1 2.1 collective-permute-start.2
  3.2 3.6 %collective-permute-start.1 = (bf16[2,128,512]{2,1,0:T(8,128)(2,1)S(1)}, bf16[2,128,512]{2,1,0:T(8,128)(2,1)S(1)}, u32[]{:S(2)}, u32[]{:S(2)}) collective-permute-start(bf16[2,128,512]{2,1,0:T(8,128)(2,1)S(1)} %bitcast.36), channel_id=1, source_target_pairs={{0,2},{1,3},{2,0},{3,1},{4,6},{5,7},{6,4},{7,5},{8,10},{9,11},{10,... | collective-permute-start | bytes 786440 | tf_op jit(solution)/shard_map/ppermute | solution.py:499
  11.6 6.8 %collective-permute-done.1.i2.m2 = bf16[2,128,512]{2,1,0:T(8,128)(2,1)S(1)} collective-permute-done((bf16[2,128,512]{2,1,0:T(8,128)(2,1)S(1)}, bf16[2,128,512]{2,1,0:T(8,128)(2,1)S(1)}, u32[]{:S(2)}, u32[]{:S(2)}) %collective-permute-start.1) | collective-permute-done | bytes 262176 | tf_op jit(solution)/shard_map/ppermute | solution.py:499
  18.4 1.7 copy-done.2
  20.1 3.7 %states.1 = (f32[16,128,128]{2,1,0:T(8,128)S(1)}, bf16[32,72,128]{2,1,0:T(8,128)(2,1)}) custom-call(s32[32]{0:T(128)S(1)} %fusion.slot_ref, bf16[512,2048]{1,0:T(8,128)(2,1)S(1)} %copy-done.2, f32[4,32,512]{2,1,0:T(8,128)S(1)} %prep.1.prep_ref, bf16[2,128,512]{2,1,0:T(8,128)(2,1)S(1)} %bitcast.38, bf16[2,128,512]{2,1,0:T(8,128)(2,1)S(1)} %collective-permute-done.i1.m1, ...), custom_call_target="tpu_custom_call" | custom-call | flops 600000000 | bytes 5000000 | tf_op jit(solution)/shard_map/states/pallas_call | solution.py:525
  24.9 7.4 %all-to-all-start = ((bf16[32,72,128]{2,1,0:T(8,128)(2,1)}), bf16[32,72,128]{2,1,0:T(8,128)(2,1)S(1)}, u32[]{:S(2)}, u32[]{:S(2)}) async-start(bf16[32,72,128]{2,1,0:T(8,128)(2,1)} %get-tuple-element.22), calls=%async_computation | async-start | bytes 1179648 | tf_op jit(solution)/shard_map/all_to_all | solution.py:556
  32.4 1.2 collective-permute-start.5
  33.6 2.4 collective-permute-start.4
  36.0 1.2 collective-permute-start.3
  38.0 6.2 %all-to-all-done.in_ref = bf16[32,72,128]{2,1,0:T(8,128)(2,1)S(1)} async-done(((bf16[32,72,128]{2,1,0:T(8,128)(2,1)}), bf16[32,72,128]{2,1,0:T(8,128)(2,1)S(1)}, u32[]{:S(2)}, u32[]{:S(2)}) %all-to-all-start) | async-done | bytes 589856 | tf_op jit(solution)/shard_map/all_to_all | solution.py:556
  45.1 4.1 %all-to-all-start.1 = ((bf16[32,64,128]{2,1,0:T(8,128)(2,1)}), bf16[32,64,128]{2,1,0:T(8,128)(2,1)S(1)}, u32[]{:S(2)}, u32[]{:S(2)}) async-start(bf16[32,64,128]{2,1,0:T(8,128)(2,1)} %scan.1), calls=%async_computation.1 | async-start | bytes 1048576 | tf_op jit(solution)/shard_map/all_to_all | solution.py:563
  51.1 8.3 %within.1.within_ref = bf16[512,2048]{1,0:T(8,128)(2,1)} custom-call(s32[32]{0:T(128)} %copy-done.12, bf16[512,2048]{1,0:T(8,128)(2,1)} %x_ref.3, f32[4,32,512]{2,1,0:T(8,128)} %copy-done.4, f32[1,2048]{1,0:T(1,128)} %broadcast_in_dim_reshape.3.skip_ref, bf16[2,128,512]{2,1,0:T(8,128)(2,1)} %bitcast.39, bf16[2,128,512]{2,1,0:T(8,128)(2,1)} %copy-done.9, ...), custom_call_target="tpu_custom_call" | custom-call | flops 12000000000 | bytes 8000000 | tf_op jit(solution)/shard_map/within/pallas_call | solution.py:566
  61.2 12.8 %project.1 = (bf16[128,2048]{1,0:T(8,128)(2,1)}, bf16[128,2048]{1,0:T(8,128)(2,1)}, bf16[128,2048]{1,0:T(8,128)(2,1)}, bf16[128,2048]{1,0:T(8,128)(2,1)}) custom-call(s32[32]{0:T(128)} %copy-done.12, s32[1]{0:T(128)} %bitcast.place_ref, bf16[512,2048]{1,0:T(8,128)(2,1)} %within.1.within_ref, f32[4,32,512]{2,1,0:T(8,128)} %copy-done.4, f32[1,2048]{1,0:T(1,128)} %bitcast.65, ...), custom_call_target="tpu_custom_call" | custom-call | flops 6000000000 | bytes 16000000 | tf_op jit(solution)/shard_map/project/pallas_call | solution.py:586
  75.2 2.4 collective-permute-start.8
  77.6 1.5 collective-permute-start.9
  79.8 10.3 %collective-permute-done.7.prev_ref = bf16[128,2048]{1,0:T(8,128)(2,1)S(1)} collective-permute-done((bf16[128,2048]{1,0:T(8,128)(2,1)}, bf16[128,2048]{1,0:T(8,128)(2,1)S(1)}, u32[]{:S(2)}, u32[]{:S(2)}) %collective-permute-start.7) | collective-permute-done | bytes 524320 | tf_op jit(solution)/shard_map/ppermute | solution.py:609
  90.0 11.5 %collective-permute-done.8.far_ref = bf16[128,2048]{1,0:T(8,128)(2,1)S(1)} collective-permute-done((bf16[128,2048]{1,0:T(8,128)(2,1)}, bf16[128,2048]{1,0:T(8,128)(2,1)S(1)}, u32[]{:S(2)}, u32[]{:S(2)}) %collective-permute-start.8) | collective-permute-done | bytes 524320 | tf_op jit(solution)/shard_map/ppermute | solution.py:610
  103.0 3.9 %tokens.1 = (f32[128,2048]{1,0:T(8,128)S(1)}, bf16[2,256,448]{2,1,0:T(8,128)(2,1)S(1)}, bf16[3584,256]{1,0:T(8,128)(2,1)S(1)}, bf16[3584,256]{1,0:T(8,128)(2,1)}) custom-call(bf16[128,2048]{1,0:T(8,128)(2,1)S(1)} %copy-done.14, bf16[128,2048]{1,0:T(8,128)(2,1)S(1)} %copy-done.16, bf16[128,2048]{1,0:T(8,128)(2,1)S(1)} %collective-permute-done.7.prev_ref, ...), custom_call_target="tpu_custom_call" | custom-call | flops 1000000000 | bytes 8000000 | tf_op jit(solution)/shard_map/tokens/pallas_call | solution.py:620
  106.9 35.6 %all_to_all.30 = bf16[448,8,256]{2,1,0:T(8,128)(2,1)} all-to-all(bf16[448,8,256]{2,1,0:T(8,128)(2,1)S(1)} %bitcast.34), channel_id=1, replica_groups={{0,1,2,3,8,9,10,11,16,17,18,19,24,25,26,27,32,33,34,35,40,41,42,43,48,4..., dimensions={0} | all-to-all | bytes 3670016 | tf_op jit(solution)/shard_map/all_to_all | solution.py:640
  142.5 5.0 %all-to-all-start.4 = ((bf16[448,8,256]{2,1,0:T(8,128)(2,1)}), bf16[448,8,256]{2,1,0:T(8,128)(2,1)S(1)}, u32[]{:S(2)}, u32[]{:S(2)}) async-start(bf16[448,8,256]{2,1,0:T(8,128)(2,1)} %bitcast.20), calls=%async_computation.4 | async-start | bytes 3670016 | tf_op jit(solution)/shard_map/all_to_all | solution.py:640
  147.5 18.5 %experts.2 = bf16[3584,256]{1,0:T(8,128)(2,1)} custom-call(bf16[3584,256]{1,0:T(8,128)(2,1)} %bitcast.46, bf16[2048,1024]{1,0:T(8,128)(2,1)} %bitcast.57, bf16[2048,1024]{1,0:T(8,128)(2,1)} %bitcast.60, bf16[1024,2048]{1,0:T(8,128)(2,1)} %bitcast.63, bf16[2048,1024]{1,0:T(8,128)(2,1)} %collective-permute-done.6.g1, ...), custom_call_target="tpu_custom_call" | custom-call | flops 11274289152 | bytes 28000000 | tf_op jit(solution)/shard_map/experts/pallas_call | solution.py:689
  166.0 8.1 %all-to-all-done.4 = bf16[448,8,256]{2,1,0:T(8,128)(2,1)S(1)} async-done(((bf16[448,8,256]{2,1,0:T(8,128)(2,1)}), bf16[448,8,256]{2,1,0:T(8,128)(2,1)S(1)}, u32[]{:S(2)}, u32[]{:S(2)}) %all-to-all-start.4) | async-done | bytes 1835040 | tf_op jit(solution)/shard_map/all_to_all | solution.py:640
  174.1 1.2 copy-done.17
  175.3 14.1 %all-to-all-start.3 = ((bf16[448,8,256]{2,1,0:T(8,128)(2,1)}), bf16[448,8,256]{2,1,0:T(8,128)(2,1)S(1)}, u32[]{:S(2)}, u32[]{:S(2)}) async-start(bf16[448,8,256]{2,1,0:T(8,128)(2,1)} %bitcast.45), calls=%async_computation.3 | async-start | bytes 3670016 | tf_op jit(solution)/shard_map/all_to_all | solution.py:640
  189.5 18.5 %experts.3 = bf16[3584,256]{1,0:T(8,128)(2,1)} custom-call(bf16[3584,256]{1,0:T(8,128)(2,1)} %bitcast.43, bf16[2048,1024]{1,0:T(8,128)(2,1)} %bitcast.58, bf16[2048,1024]{1,0:T(8,128)(2,1)} %bitcast.61, bf16[1024,2048]{1,0:T(8,128)(2,1)} %bitcast.64, bf16[2048,1024]{1,0:T(8,128)(2,1)} %collective-permute-done.6.g1, ...), custom_call_target="tpu_custom_call" | custom-call | flops 11274289152 | bytes 28000000 | tf_op jit(solution)/shard_map/experts/pallas_call | solution.py:689
  207.9 7.7 %all-to-all-done.3 = bf16[448,8,256]{2,1,0:T(8,128)(2,1)S(1)} async-done(((bf16[448,8,256]{2,1,0:T(8,128)(2,1)}), bf16[448,8,256]{2,1,0:T(8,128)(2,1)S(1)}, u32[]{:S(2)}, u32[]{:S(2)}) %all-to-all-start.3) | async-done | bytes 1835040 | tf_op jit(solution)/shard_map/all_to_all | solution.py:640
  215.6 1.3 copy-done
  216.9 5.2 %all-to-all-start.5 = ((bf16[448,8,256]{2,1,0:T(8,128)(2,1)}), bf16[448,8,256]{2,1,0:T(8,128)(2,1)S(1)}, u32[]{:S(2)}, u32[]{:S(2)}) async-start(bf16[448,8,256]{2,1,0:T(8,128)(2,1)} %bitcast.44), calls=%async_computation.5 | async-start | bytes 3670016 | tf_op jit(solution)/shard_map/all_to_all | solution.py:640
  222.1 1.5 copy-done.1
  223.6 1.2 copy-done.6
  225.9 22.7 %all-to-all-done.5 = bf16[448,8,256]{2,1,0:T(8,128)(2,1)S(1)} async-done(((bf16[448,8,256]{2,1,0:T(8,128)(2,1)}), bf16[448,8,256]{2,1,0:T(8,128)(2,1)S(1)}, u32[]{:S(2)}, u32[]{:S(2)}) %all-to-all-start.5) | async-done | bytes 1835040 | tf_op jit(solution)/shard_map/all_to_all | solution.py:640
  248.5 1.8 combine.3
  (78 shorter events, 16.6 us)
Async XLA Ops:
  1.1 23.8 %copy-start.3 = (bf16[512,2,128]{0,2,1:T(8,128)(2,1)}, bf16[512,2,128]{0,2,1:T(8,128)(2,1)S(1)}, u32[]{:S(2)}) copy-start(bf16[512,2,128]{0,2,1:T(8,128)(2,1)S(1)} %copy.24) | copy-start | bytes 786436
  1.1 10.5 %collective-permute-start.2 = (bf16[2,128,512]{2,1,0:T(8,128)(2,1)S(1)}, bf16[2,128,512]{2,1,0:T(8,128)(2,1)S(1)}, u32[]{:S(2)}, u32[]{:S(2)}) collective-permute-start(bf16[2,128,512]{2,1,0:T(8,128)(2,1)S(1)} %bitcast.35), channel_id=1, source_target_pairs={{0,1},{1,2},{2,3},{3,0},{4,5},{5,6},{6,7},{7,4},{8,9},{9,10},{10,1... | collective-permute-start | bytes 786440 | tf_op jit(solution)/shard_map/ppermute | solution.py:500
  3.2 15.2 %collective-permute-start.1 = (bf16[2,128,512]{2,1,0:T(8,128)(2,1)S(1)}, bf16[2,128,512]{2,1,0:T(8,128)(2,1)S(1)}, u32[]{:S(2)}, u32[]{:S(2)}) collective-permute-start(bf16[2,128,512]{2,1,0:T(8,128)(2,1)S(1)} %bitcast.36), channel_id=1, source_target_pairs={{0,2},{1,3},{2,0},{3,1},{4,6},{5,7},{6,4},{7,5},{8,10},{9,11},{10,... | collective-permute-start | bytes 786440 | tf_op jit(solution)/shard_map/ppermute | solution.py:499
  6.8 11.6 %collective-permute-start = (bf16[2,128,512]{2,1,0:T(8,128)(2,1)S(1)}, bf16[2,128,512]{2,1,0:T(8,128)(2,1)S(1)}, u32[]{:S(2)}, u32[]{:S(2)}) collective-permute-start(bf16[2,128,512]{2,1,0:T(8,128)(2,1)S(1)} %bitcast.37), channel_id=1, source_target_pairs={{0,3},{1,0},{2,1},{3,2},{4,7},{5,4},{6,5},{7,6},{8,11},{9,8},{10,9... | collective-permute-start | bytes 786440 | tf_op jit(solution)/shard_map/ppermute | solution.py:500
  10.2 22.2 %copy-start.19 = (bf16[512,2,128]{2,1,0:T(2,128)(2,1)S(1)}, bf16[512,2,128]{2,1,0:T(2,128)(2,1)}, u32[]{:S(2)}) copy-start(bf16[512,2,128]{2,1,0:T(2,128)(2,1)} %param.22) | copy-start | bytes 786436
  10.5 14.4 %copy-start.4 = (f32[4,32,512]{2,1,0:T(8,128)}, f32[4,32,512]{2,1,0:T(8,128)S(1)}, u32[]{:S(2)}) copy-start(f32[4,32,512]{2,1,0:T(8,128)S(1)} %prep.1.prep_ref) | copy-start | bytes 786436
  10.5 26.8 %copy-start.23 = (f32[32]{0:T(128)S(1)}, f32[32]{0:T(128)}, u32[]{:S(2)}) copy-start(f32[32]{0:T(128)} %param.24) | copy-start | bytes 388
  11.2 13.6 %copy-start.12 = (s32[32]{0:T(128)}, s32[32]{0:T(128)S(1)}, u32[]{:S(2)}) copy-start(s32[32]{0:T(128)S(1)} %fusion.slot_ref) | copy-start | bytes 388
  11.6 13.3 %copy-start.7 = (bf16[2,128,512]{2,1,0:T(8,128)(2,1)}, bf16[2,128,512]{2,1,0:T(8,128)(2,1)S(1)}, u32[]{:S(2)}) copy-start(bf16[2,128,512]{2,1,0:T(8,128)(2,1)S(1)} %collective-permute-done.2.i3.m3) | copy-start | bytes 786436
  18.4 6.5 %copy-start.8 = (bf16[2,128,512]{2,1,0:T(8,128)(2,1)}, bf16[2,128,512]{2,1,0:T(8,128)(2,1)S(1)}, u32[]{:S(2)}) copy-start(bf16[2,128,512]{2,1,0:T(8,128)(2,1)S(1)} %collective-permute-done.1.i2.m2) | copy-start | bytes 786436
  18.4 1.7 copy-start.2
  20.1 4.8 %copy-start.9 = (bf16[2,128,512]{2,1,0:T(8,128)(2,1)}, bf16[2,128,512]{2,1,0:T(8,128)(2,1)S(1)}, u32[]{:S(2)}) copy-start(bf16[2,128,512]{2,1,0:T(8,128)(2,1)S(1)} %collective-permute-done.i1.m1) | copy-start | bytes 786436
  24.9 34.5 %collective-permute-start.6 = (bf16[2048,1024]{1,0:T(8,128)(2,1)}, bf16[2048,1024]{1,0:T(8,128)(2,1)}, u32[]{:S(2)}, u32[]{:S(2)}) collective-permute-start(bf16[2048,1024]{1,0:T(8,128)(2,1)} %bitcast.56), channel_id=1, source_target_pairs={{0,4},{4,0},{8,12},{12,8},{16,20},{20,16},{24,28},{28,24},{32,36},... | collective-permute-start | bytes 12582920 | tf_op jit(solution)/shard_map/ppermute | solution.py:552
  24.9 19.3 %all-to-all-start = ((bf16[32,72,128]{2,1,0:T(8,128)(2,1)}), bf16[32,72,128]{2,1,0:T(8,128)(2,1)S(1)}, u32[]{:S(2)}, u32[]{:S(2)}) async-start(bf16[32,72,128]{2,1,0:T(8,128)(2,1)} %get-tuple-element.22), calls=%async_computation | async-start | bytes 1179648 | tf_op jit(solution)/shard_map/all_to_all | solution.py:556
  32.4 17.2 %copy-start.21 = (bf16[512,2,128]{2,0,1:T(8,128)(2,1)}, bf16[512,2,128]{2,0,1:T(8,128)(2,1)S(1)}, u32[]{:S(2)}) copy-start(bf16[512,2,128]{2,0,1:T(8,128)(2,1)S(1)} %copy.32) | copy-start | bytes 786436
  32.4 16.8 %collective-permute-start.5 = (bf16[2,512,128]{2,1,0:T(8,128)(2,1)S(1)}, bf16[2,512,128]{2,1,0:T(8,128)(2,1)S(1)}, u32[]{:S(2)}, u32[]{:S(2)}) collective-permute-start(bf16[2,512,128]{2,1,0:T(8,128)(2,1)S(1)} %bitcast.50), channel_id=1, source_target_pairs={{0,1},{1,2},{2,3},{3,0},{4,5},{5,6},{6,7},{7,4},{8,9},{9,10},{10,1... | collective-permute-start | bytes 786440 | tf_op jit(solution)/shard_map/ppermute | solution.py:500
  33.6 16.0 %collective-permute-start.4 = (bf16[2,512,128]{2,1,0:T(8,128)(2,1)S(1)}, bf16[2,512,128]{2,1,0:T(8,128)(2,1)S(1)}, u32[]{:S(2)}, u32[]{:S(2)}) collective-permute-start(bf16[2,512,128]{2,1,0:T(8,128)(2,1)S(1)} %bitcast.51), channel_id=1, source_target_pairs={{0,2},{1,3},{2,0},{3,1},{4,6},{5,7},{6,4},{7,5},{8,10},{9,11},{10,... | collective-permute-start | bytes 786440 | tf_op jit(solution)/shard_map/ppermute | solution.py:499
  36.0 13.6 %collective-permute-start.3 = (bf16[2,512,128]{2,1,0:T(8,128)(2,1)S(1)}, bf16[2,512,128]{2,1,0:T(8,128)(2,1)S(1)}, u32[]{:S(2)}, u32[]{:S(2)}) collective-permute-start(bf16[2,512,128]{2,1,0:T(8,128)(2,1)S(1)} %bitcast.52), channel_id=1, source_target_pairs={{0,3},{1,0},{2,1},{3,2},{4,7},{5,4},{6,5},{7,6},{8,11},{9,8},{10,9... | collective-permute-start | bytes 786440 | tf_op jit(solution)/shard_map/ppermute | solution.py:500
  37.3 110.2 %collective-permute-start.10 = (bf16[2048,1024]{1,0:T(8,128)(2,1)}, bf16[2048,1024]{1,0:T(8,128)(2,1)}, u32[]{:S(2)}, u32[]{:S(2)}) collective-permute-start(bf16[2048,1024]{1,0:T(8,128)(2,1)} %bitcast.59), channel_id=1, source_target_pairs={{0,4},{4,0},{8,12},{12,8},{16,20},{20,16},{24,28},{28,24},{32,36},... | collective-permute-start | bytes 12582920 | tf_op jit(solution)/shard_map/ppermute | solution.py:553
  45.1 15.3 %all-to-all-start.1 = ((bf16[32,64,128]{2,1,0:T(8,128)(2,1)}), bf16[32,64,128]{2,1,0:T(8,128)(2,1)S(1)}, u32[]{:S(2)}, u32[]{:S(2)}) async-start(bf16[32,64,128]{2,1,0:T(8,128)(2,1)} %scan.1), calls=%async_computation.1 | async-start | bytes 1048576 | tf_op jit(solution)/shard_map/all_to_all | solution.py:563
  49.3 98.3 %collective-permute-start.11 = (bf16[1024,2048]{1,0:T(8,128)(2,1)}, bf16[1024,2048]{1,0:T(8,128)(2,1)}, u32[]{:S(2)}, u32[]{:S(2)}) collective-permute-start(bf16[1024,2048]{1,0:T(8,128)(2,1)} %bitcast.62), channel_id=1, source_target_pairs={{0,4},{4,0},{8,12},{12,8},{16,20},{20,16},{24,28},{28,24},{32,36},... | collective-permute-start | bytes 12582920 | tf_op jit(solution)/shard_map/ppermute | solution.py:554
  61.2 17.9 %copy-start.22 = (s32[128,4]{0,1:T(4,128)S(1)}, s32[128,4]{0,1:T(4,128)}, u32[]{:S(2)}) copy-start(s32[128,4]{0,1:T(4,128)} %param.30) | copy-start | bytes 6148
  61.2 18.0 %copy-start.20 = (bf16[2048,64]{0,1:T(8,128)(2,1)S(1)}, bf16[2048,64]{0,1:T(8,128)(2,1)}, u32[]{:S(2)}) copy-start(bf16[2048,64]{0,1:T(8,128)(2,1)} %param.29) | copy-start | bytes 786436
  61.2 40.7 %copy-start.14 = (bf16[128,2048]{1,0:T(8,128)(2,1)S(1)}, bf16[128,2048]{1,0:T(8,128)(2,1)}, u32[]{:S(2)}) copy-start(bf16[128,2048]{1,0:T(8,128)(2,1)} %residual_ref.1) | copy-start | bytes 1572868
  61.2 40.7 %copy-start.15 = (f32[2048]{0:T(1024)S(1)}, f32[2048]{0:T(1024)}, u32[]{:S(2)}) copy-start(f32[2048]{0:T(1024)} %param.28) | copy-start | bytes 24580
  74.1 16.0 %collective-permute-start.7 = (bf16[128,2048]{1,0:T(8,128)(2,1)}, bf16[128,2048]{1,0:T(8,128)(2,1)S(1)}, u32[]{:S(2)}, u32[]{:S(2)}) collective-permute-start(bf16[128,2048]{1,0:T(8,128)(2,1)} %get-tuple-element.25), channel_id=1, source_target_pairs={{0,1},{1,2},{2,3},{3,0},{4,5},{5,6},{6,7},{7,4},{8,9},{9,10},{10,1... | collective-permute-start | bytes 1572872 | tf_op jit(solution)/shard_map/ppermute | solution.py:609
  75.2 26.3 %collective-permute-start.8 = (bf16[128,2048]{1,0:T(8,128)(2,1)}, bf16[128,2048]{1,0:T(8,128)(2,1)S(1)}, u32[]{:S(2)}, u32[]{:S(2)}) collective-permute-start(bf16[128,2048]{1,0:T(8,128)(2,1)} %get-tuple-element.26), channel_id=1, source_target_pairs={{0,2},{1,3},{2,0},{3,1},{4,6},{5,7},{6,4},{7,5},{8,10},{9,11},{10,... | collective-permute-start | bytes 1572872 | tf_op jit(solution)/shard_map/ppermute | solution.py:610
  77.6 24.3 %collective-permute-start.9 = (bf16[128,2048]{1,0:T(8,128)(2,1)}, bf16[128,2048]{1,0:T(8,128)(2,1)S(1)}, u32[]{:S(2)}, u32[]{:S(2)}) collective-permute-start(bf16[128,2048]{1,0:T(8,128)(2,1)} %get-tuple-element.27), channel_id=1, source_target_pairs={{0,3},{1,0},{2,1},{3,2},{4,7},{5,4},{6,5},{7,6},{8,11},{9,8},{10,9... | collective-permute-start | bytes 1572872 | tf_op jit(solution)/shard_map/ppermute | solution.py:611
  106.9 35.6 %copy-start.5 = (f32[128,2048]{1,0:T(8,128)}, f32[128,2048]{1,0:T(8,128)S(1)}, u32[]{:S(2)}) copy-start(f32[128,2048]{1,0:T(8,128)S(1)} %get-tuple-element.28.base_ref) | copy-start | bytes 3145732
  142.5 31.6 %all-to-all-start.4 = ((bf16[448,8,256]{2,1,0:T(8,128)(2,1)}), bf16[448,8,256]{2,1,0:T(8,128)(2,1)S(1)}, u32[]{:S(2)}, u32[]{:S(2)}) async-start(bf16[448,8,256]{2,1,0:T(8,128)(2,1)} %bitcast.20), calls=%async_computation.4 | async-start | bytes 3670016 | tf_op jit(solution)/shard_map/all_to_all | solution.py:640
  175.3 40.3 %all-to-all-start.3 = ((bf16[448,8,256]{2,1,0:T(8,128)(2,1)}), bf16[448,8,256]{2,1,0:T(8,128)(2,1)S(1)}, u32[]{:S(2)}, u32[]{:S(2)}) async-start(bf16[448,8,256]{2,1,0:T(8,128)(2,1)} %bitcast.45), calls=%async_computation.3 | async-start | bytes 3670016 | tf_op jit(solution)/shard_map/all_to_all | solution.py:640
  216.9 31.7 %all-to-all-start.5 = ((bf16[448,8,256]{2,1,0:T(8,128)(2,1)}), bf16[448,8,256]{2,1,0:T(8,128)(2,1)S(1)}, u32[]{:S(2)}, u32[]{:S(2)}) async-start(bf16[448,8,256]{2,1,0:T(8,128)(2,1)} %bitcast.44), calls=%async_computation.5 | async-start | bytes 3670016 | tf_op jit(solution)/shard_map/all_to_all | solution.py:640
  (12 other events, 11.9 us)
where the time goes:
time: 254 us; the launch traced here: 251 us
  waiting for transfers between devices  74.9 us (29%)
  Pallas kernels  69.8 us (27%)
  starting transfers between devices  52.8 us (21%)
  blocking collectives  35.6 us (14%)
  local copies, waits for them, and re-layouts  16.2 us (6%)
    all_to_all x3, waiting for transfers between devices, swap(): lax.all_to_all(rows.reshape(count, ROW, CELL), ('seq', 'exp'), split_axis...  38.4 us
    pallas_call x2, Pallas kernels, body(): run_experts(rows, w_gate[0], w_up[0], w_down[0], other_gate, other_up, ot...  36.9 us
    all_to_all x1, blocking collectives, swap(): lax.all_to_all(rows.reshape(count, ROW, CELL), ('seq', 'exp'), split_axis...  35.6 us
    all_to_all x3, starting transfers between devices, swap(): lax.all_to_all(rows.reshape(count, ROW, CELL), ('seq', 'exp'), split_axis...  24.3 us
    unnamed x57, local copies, waits for them, and re-layouts  14.1 us
    pallas_call x1, Pallas kernels, body(): pl.pallas_call(project_kernel, grid_spec=pltpu.PrefetchScalarGridSpec(num...  12.8 us
    ppermute x1, waiting for transfers between devices, body(): from_far = lax.ppermute(far, 'exp', opposite)  11.5 us
    ppermute x1, waiting for transfers between devices, body(): from_prev = lax.ppermute(up, 'exp', nxt)  10.3 us
  transfers between devices with their start and end apart: 17, of which 10 were waited for; matrix products, arithmetic and copies ran while one was open for 1% of the time, Pallas kernels for 26%

commit v1 on v0

--- a/solution.py
+++ b/solution.py
@@ -133,7 +133,7 @@
             )
             for e in (BLOCK, 2 * BLOCK)
         ]
-        fresh_all[step * STEP_PAIRS + p] = fresh[0]
+        fresh_all[step * STEP_PAIRS + p] = fresh[0].astype(BF16)
         final = (ends[1] * fresh[0] + fresh[1]).astype(BF16)
         decay = ends[0] * ends[1]
         high = decay.astype(BF16).astype(F32)
@@ -257,7 +257,7 @@
             prep_ref[3, 2 * p : 2 * p + 1, BLOCK - 1 : BLOCK], prep_ref[3, 2 * p + 1 : 2 * p + 2, BLOCK - 1 : BLOCK]
         )
         arriving = enter_ref[p].astype(F32)
-        entering = [arriving, first_end * arriving + fresh_ref[p]]
+        entering = [arriving, first_end * arriving + fresh_ref[p].astype(F32)]
         for b in range(2):
             rows = slice(b * BLOCK, (b + 1) * BLOCK)
             left = jnp.concatenate([maps[slots[0], rows, :], maps[slots[1], rows, :]], axis=1)
@@ -310,8 +310,8 @@
     residual_ref,
     own_ref,
     prev_ref,
+    next_ref,
     far_ref,
-    next_ref,
     gain_ref,
     router_ref,
     ids_ref,
@@ -531,14 +531,14 @@
             out_specs=[pl.BlockSpec(memory_space=pltpu.HBM)] * 2,
             scratch_shapes=[
                 pltpu.VMEM((G, NST, length), BF16),
-                pltpu.VMEM((heads // 2, NST, PAIR), F32),
+                pltpu.VMEM((heads // 2, NST, PAIR), BF16),
                 pltpu.VMEM((heads, 72, PAIR), BF16),
                 pltpu.SemaphoreType.DMA((steps,)),
                 pltpu.SemaphoreType.DMA((steps,)),
             ],
         ),
         out_shape=[
-            jax.ShapeDtypeStruct((heads // 2, NST, PAIR), F32),
+            jax.ShapeDtypeStruct((heads // 2, NST, PAIR), BF16),
             jax.ShapeDtypeStruct((heads, 72, PAIR), BF16),
         ],
         compiler_params=params(16),
@@ -607,8 +607,8 @@
     )(slot, me[None].astype(jnp.int32), within, prep, gain_lanes, entering, fresh, *out_maps, w_out)
 
     from_prev = lax.ppermute(up, "exp", nxt)
+    from_next = lax.ppermute(down, "exp", prv)
     from_far = lax.ppermute(far, "exp", opposite)
-    from_next = lax.ppermute(down, "exp", prv)
 
     experts = w_router.shape[1]
     per_group = experts // ring
@@ -630,7 +630,7 @@
             flops=1_000_000_000, bytes_accessed=8_000_000, transcendentals=0
         ),
         name="tokens",
-    )(residual, own, from_prev, from_far, from_next, moe_gain[None, :], router, expert_ids)
+    )(residual, own, from_prev, from_next, from_far, moe_gain[None, :], router, expert_ids)
 
     cores = [
         [(c // ring * 2 + h) * ring + c % ring for c in range(experts)] for h in range(2)

time: 254 us -> 253 us (level)
    ppermute x1, waiting for transfers between devices: 11.5 us -> 0.86 us  [body(): from_far = lax.ppermute(far, 'exp', opposite)]
    ppermute x1, waiting for transfers between devices: 0.35 us -> 10.7 us  [body(): from_next = lax.ppermute(down, 'exp', prv)]
where the time goes in v1:
time: 253 us; the launch traced here: 248 us
  waiting for transfers between devices  73 us (29%)
  Pallas kernels  70.2 us (28%)
  starting transfers between devices  53.6 us (21%)
  blocking collectives  34.2 us (14%)
  local copies, waits for them, and re-layouts  16 us (6%)
    pallas_call x2, Pallas kernels, body(): run_experts(rows, w_gate[0], w_up[0], w_down[0], other_gate, other_up, ot...  36.9 us
    all_to_all x3, waiting for transfers between devices, swap(): lax.all_to_all(rows.reshape(count, ROW, CELL), ('seq', 'exp'), split_axis...  36.2 us
    all_to_all x1, blocking collectives, swap(): lax.all_to_all(rows.reshape(count, ROW, CELL), ('seq', 'exp'), split_axis...  34.2 us
    all_to_all x3, starting transfers between devices, swap(): lax.all_to_all(rows.reshape(count, ROW, CELL), ('seq', 'exp'), split_axis...  25.8 us
    unnamed x57, local copies, waits for them, and re-layouts  13.9 us
    pallas_call x1, Pallas kernels, body(): pl.pallas_call(project_kernel, grid_spec=pltpu.PrefetchScalarGridSpec(num...  12.8 us
    ppermute x1, waiting for transfers between devices, body(): from_prev = lax.ppermute(up, 'exp', nxt)  10.9 us
    ppermute x1, waiting for transfers between devices, body(): from_next = lax.ppermute(down, 'exp', prv)  10.7 us
  transfers between devices with their start and end apart: 17, of which 10 were waited for; matrix products, arithmetic and copies ran while one was open for 1% of the time, Pallas kernels for 26%

profile of v1, /device:TPU:0, one launch (start us, length us, event | category | flops | bytes accessed | tf_op | source)
XLA Modules:
  0.0 248.2 jit_solution(7098145721519781704)
XLA Ops:
  1.1 2.1 collective-permute-start.2
  3.2 3.6 %collective-permute-start.1 = (bf16[2,128,512]{2,1,0:T(8,128)(2,1)S(1)}, bf16[2,128,512]{2,1,0:T(8,128)(2,1)S(1)}, u32[]{:S(2)}, u32[]{:S(2)}) collective-permute-start(bf16[2,128,512]{2,1,0:T(8,128)(2,1)S(1)} %bitcast.36), channel_id=1, source_target_pairs={{0,2},{1,3},{2,0},{3,1},{4,6},{5,7},{6,4},{7,5},{8,10},{9,11},{10,... | collective-permute-start | bytes 786440 | tf_op jit(solution)/shard_map/ppermute | solution.py:499
  11.6 6.8 %collective-permute-done.1.i2.m2 = bf16[2,128,512]{2,1,0:T(8,128)(2,1)S(1)} collective-permute-done((bf16[2,128,512]{2,1,0:T(8,128)(2,1)S(1)}, bf16[2,128,512]{2,1,0:T(8,128)(2,1)S(1)}, u32[]{:S(2)}, u32[]{:S(2)}) %collective-permute-start.1) | collective-permute-done | bytes 262176 | tf_op jit(solution)/shard_map/ppermute | solution.py:499
  18.4 1.7 copy-done.2
  20.1 4.2 %states.1 = (bf16[16,128,128]{2,1,0:T(8,128)(2,1)S(1)}, bf16[32,72,128]{2,1,0:T(8,128)(2,1)}) custom-call(s32[32]{0:T(128)S(1)} %fusion.slot_ref, bf16[512,2048]{1,0:T(8,128)(2,1)S(1)} %copy-done.2, f32[4,32,512]{2,1,0:T(8,128)S(1)} %prep.1.prep_ref, bf16[2,128,512]{2,1,0:T(8,128)(2,1)S(1)} %bitcast.38, bf16[2,128,512]{2,1,0:T(8,128)(2,1)S(1)} %collective-permute-done.i1.m1, ...), custom_call_target="tpu_custom_call" | custom-call | flops 600000000 | bytes 5000000 | tf_op jit(solution)/shard_map/states/pallas_call | solution.py:525
  25.2 7.4 %all-to-all-start = ((bf16[32,72,128]{2,1,0:T(8,128)(2,1)}), bf16[32,72,128]{2,1,0:T(8,128)(2,1)S(1)}, u32[]{:S(2)}, u32[]{:S(2)}) async-start(bf16[32,72,128]{2,1,0:T(8,128)(2,1)} %get-tuple-element.22), calls=%async_computation | async-start | bytes 1179648 | tf_op jit(solution)/shard_map/all_to_all | solution.py:556
  32.7 1.2 collective-permute-start.5
  33.9 2.4 collective-permute-start.4
  36.3 1.2 collective-permute-start.3
  38.3 6.2 %all-to-all-done.in_ref = bf16[32,72,128]{2,1,0:T(8,128)(2,1)S(1)} async-done(((bf16[32,72,128]{2,1,0:T(8,128)(2,1)}), bf16[32,72,128]{2,1,0:T(8,128)(2,1)S(1)}, u32[]{:S(2)}, u32[]{:S(2)}) %all-to-all-start) | async-done | bytes 589856 | tf_op jit(solution)/shard_map/all_to_all | solution.py:556
  45.3 4.1 %all-to-all-start.1 = ((bf16[32,64,128]{2,1,0:T(8,128)(2,1)}), bf16[32,64,128]{2,1,0:T(8,128)(2,1)S(1)}, u32[]{:S(2)}, u32[]{:S(2)}) async-start(bf16[32,64,128]{2,1,0:T(8,128)(2,1)} %scan.1), calls=%async_computation.1 | async-start | bytes 1048576 | tf_op jit(solution)/shard_map/all_to_all | solution.py:563
  51.3 8.3 %within.1.within_ref = bf16[512,2048]{1,0:T(8,128)(2,1)} custom-call(s32[32]{0:T(128)} %copy-done.12, bf16[512,2048]{1,0:T(8,128)(2,1)} %x_ref.3, f32[4,32,512]{2,1,0:T(8,128)} %copy-done.4, f32[1,2048]{1,0:T(1,128)} %broadcast_in_dim_reshape.3.skip_ref, bf16[2,128,512]{2,1,0:T(8,128)(2,1)} %bitcast.39, bf16[2,128,512]{2,1,0:T(8,128)(2,1)} %copy-done.9, ...), custom_call_target="tpu_custom_call" | custom-call | flops 12000000000 | bytes 8000000 | tf_op jit(solution)/shard_map/within/pallas_call | solution.py:566
  61.5 12.8 %project.1 = (bf16[128,2048]{1,0:T(8,128)(2,1)}, bf16[128,2048]{1,0:T(8,128)(2,1)}, bf16[128,2048]{1,0:T(8,128)(2,1)}, bf16[128,2048]{1,0:T(8,128)(2,1)}) custom-call(s32[32]{0:T(128)} %copy-done.12, s32[1]{0:T(128)} %bitcast.place_ref, bf16[512,2048]{1,0:T(8,128)(2,1)} %within.1.within_ref, f32[4,32,512]{2,1,0:T(8,128)} %copy-done.4, f32[1,2048]{1,0:T(1,128)} %bitcast.65, ...), custom_call_target="tpu_custom_call" | custom-call | flops 6000000000 | bytes 16000000 | tf_op jit(solution)/shard_map/project/pallas_call | solution.py:586
  75.4 2.1 collective-permute-start.8
  77.5 1.2 collective-permute-start.9
  79.3 10.9 %collective-permute-done.7.prev_ref = bf16[128,2048]{1,0:T(8,128)(2,1)S(1)} collective-permute-done((bf16[128,2048]{1,0:T(8,128)(2,1)}, bf16[128,2048]{1,0:T(8,128)(2,1)S(1)}, u32[]{:S(2)}, u32[]{:S(2)}) %collective-permute-start.7) | collective-permute-done | bytes 524320 | tf_op jit(solution)/shard_map/ppermute | solution.py:609
  90.2 10.7 %collective-permute-done.8.next_ref = bf16[128,2048]{1,0:T(8,128)(2,1)S(1)} collective-permute-done((bf16[128,2048]{1,0:T(8,128)(2,1)}, bf16[128,2048]{1,0:T(8,128)(2,1)S(1)}, u32[]{:S(2)}, u32[]{:S(2)}) %collective-permute-start.8) | collective-permute-done | bytes 524320 | tf_op jit(solution)/shard_map/ppermute | solution.py:610
  102.8 3.9 %tokens.1 = (f32[128,2048]{1,0:T(8,128)S(1)}, bf16[2,256,448]{2,1,0:T(8,128)(2,1)S(1)}, bf16[3584,256]{1,0:T(8,128)(2,1)S(1)}, bf16[3584,256]{1,0:T(8,128)(2,1)}) custom-call(bf16[128,2048]{1,0:T(8,128)(2,1)S(1)} %copy-done.13, bf16[128,2048]{1,0:T(8,128)(2,1)S(1)} %copy-done.16, bf16[128,2048]{1,0:T(8,128)(2,1)S(1)} %collective-permute-done.7.prev_ref, ...), custom_call_target="tpu_custom_call" | custom-call | flops 1000000000 | bytes 8000000 | tf_op jit(solution)/shard_map/tokens/pallas_call | solution.py:620
  106.7 34.2 %all_to_all.30 = bf16[448,8,256]{2,1,0:T(8,128)(2,1)} all-to-all(bf16[448,8,256]{2,1,0:T(8,128)(2,1)S(1)} %bitcast.34), channel_id=1, replica_groups={{0,1,2,3,8,9,10,11,16,17,18,19,24,25,26,27,32,33,34,35,40,41,42,43,48,4..., dimensions={0} | all-to-all | bytes 3670016 | tf_op jit(solution)/shard_map/all_to_all | solution.py:640
  140.9 5.5 %all-to-all-start.4 = ((bf16[448,8,256]{2,1,0:T(8,128)(2,1)}), bf16[448,8,256]{2,1,0:T(8,128)(2,1)S(1)}, u32[]{:S(2)}, u32[]{:S(2)}) async-start(bf16[448,8,256]{2,1,0:T(8,128)(2,1)} %bitcast.20), calls=%async_computation.4 | async-start | bytes 3670016 | tf_op jit(solution)/shard_map/all_to_all | solution.py:640
  146.4 18.5 %experts.2 = bf16[3584,256]{1,0:T(8,128)(2,1)} custom-call(bf16[3584,256]{1,0:T(8,128)(2,1)} %bitcast.46, bf16[2048,1024]{1,0:T(8,128)(2,1)} %bitcast.57, bf16[2048,1024]{1,0:T(8,128)(2,1)} %bitcast.60, bf16[1024,2048]{1,0:T(8,128)(2,1)} %bitcast.63, bf16[2048,1024]{1,0:T(8,128)(2,1)} %collective-permute-done.6.g1, ...), custom_call_target="tpu_custom_call" | custom-call | flops 11274289152 | bytes 28000000 | tf_op jit(solution)/shard_map/experts/pallas_call | solution.py:689
  164.9 7.2 %all-to-all-done.4 = bf16[448,8,256]{2,1,0:T(8,128)(2,1)S(1)} async-done(((bf16[448,8,256]{2,1,0:T(8,128)(2,1)}), bf16[448,8,256]{2,1,0:T(8,128)(2,1)S(1)}, u32[]{:S(2)}, u32[]{:S(2)}) %all-to-all-start.4) | async-done | bytes 1835040 | tf_op jit(solution)/shard_map/all_to_all | solution.py:640
  172.1 1.2 copy-done.17
  173.4 14.7 %all-to-all-start.3 = ((bf16[448,8,256]{2,1,0:T(8,128)(2,1)}), bf16[448,8,256]{2,1,0:T(8,128)(2,1)S(1)}, u32[]{:S(2)}, u32[]{:S(2)}) async-start(bf16[448,8,256]{2,1,0:T(8,128)(2,1)} %bitcast.45), calls=%async_computation.3 | async-start | bytes 3670016 | tf_op jit(solution)/shard_map/all_to_all | solution.py:640
  188.1 18.5 %experts.3 = bf16[3584,256]{1,0:T(8,128)(2,1)} custom-call(bf16[3584,256]{1,0:T(8,128)(2,1)} %bitcast.43, bf16[2048,1024]{1,0:T(8,128)(2,1)} %bitcast.58, bf16[2048,1024]{1,0:T(8,128)(2,1)} %bitcast.61, bf16[1024,2048]{1,0:T(8,128)(2,1)} %bitcast.64, bf16[2048,1024]{1,0:T(8,128)(2,1)} %collective-permute-done.6.g1, ...), custom_call_target="tpu_custom_call" | custom-call | flops 11274289152 | bytes 28000000 | tf_op jit(solution)/shard_map/experts/pallas_call | solution.py:689
  206.6 7.0 %all-to-all-done.3 = bf16[448,8,256]{2,1,0:T(8,128)(2,1)S(1)} async-done(((bf16[448,8,256]{2,1,0:T(8,128)(2,1)}), bf16[448,8,256]{2,1,0:T(8,128)(2,1)S(1)}, u32[]{:S(2)}, u32[]{:S(2)}) %all-to-all-start.3) | async-done | bytes 1835040 | tf_op jit(solution)/shard_map/all_to_all | solution.py:640
  213.6 1.3 copy-done
  214.8 5.6 %all-to-all-start.5 = ((bf16[448,8,256]{2,1,0:T(8,128)(2,1)}), bf16[448,8,256]{2,1,0:T(8,128)(2,1)S(1)}, u32[]{:S(2)}, u32[]{:S(2)}) async-start(bf16[448,8,256]{2,1,0:T(8,128)(2,1)} %bitcast.44), calls=%async_computation.5 | async-start | bytes 3670016 | tf_op jit(solution)/shard_map/all_to_all | solution.py:640
  220.5 1.5 copy-done.1
  222.0 1.2 copy-done.6
  224.2 22.0 %all-to-all-done.5 = bf16[448,8,256]{2,1,0:T(8,128)(2,1)S(1)} async-done(((bf16[448,8,256]{2,1,0:T(8,128)(2,1)}), bf16[448,8,256]{2,1,0:T(8,128)(2,1)S(1)}, u32[]{:S(2)}, u32[]{:S(2)}) %all-to-all-start.5) | async-done | bytes 1835040 | tf_op jit(solution)/shard_map/all_to_all | solution.py:640
  246.2 1.8 combine.3
  (78 shorter events, 16.9 us)
Async XLA Ops:
  1.1 24.0 %copy-start.3 = (bf16[512,2,128]{0,2,1:T(8,128)(2,1)}, bf16[512,2,128]{0,2,1:T(8,128)(2,1)S(1)}, u32[]{:S(2)}) copy-start(bf16[512,2,128]{0,2,1:T(8,128)(2,1)S(1)} %copy.24) | copy-start | bytes 786436
  1.1 10.5 %collective-permute-start.2 = (bf16[2,128,512]{2,1,0:T(8,128)(2,1)S(1)}, bf16[2,128,512]{2,1,0:T(8,128)(2,1)S(1)}, u32[]{:S(2)}, u32[]{:S(2)}) collective-permute-start(bf16[2,128,512]{2,1,0:T(8,128)(2,1)S(1)} %bitcast.35), channel_id=1, source_target_pairs={{0,1},{1,2},{2,3},{3,0},{4,5},{5,6},{6,7},{7,4},{8,9},{9,10},{10,1... | collective-permute-start | bytes 786440 | tf_op jit(solution)/shard_map/ppermute | solution.py:500
  3.2 15.2 %collective-permute-start.1 = (bf16[2,128,512]{2,1,0:T(8,128)(2,1)S(1)}, bf16[2,128,512]{2,1,0:T(8,128)(2,1)S(1)}, u32[]{:S(2)}, u32[]{:S(2)}) collective-permute-start(bf16[2,128,512]{2,1,0:T(8,128)(2,1)S(1)} %bitcast.36), channel_id=1, source_target_pairs={{0,2},{1,3},{2,0},{3,1},{4,6},{5,7},{6,4},{7,5},{8,10},{9,11},{10,... | collective-permute-start | bytes 786440 | tf_op jit(solution)/shard_map/ppermute | solution.py:499
  6.8 11.6 %collective-permute-start = (bf16[2,128,512]{2,1,0:T(8,128)(2,1)S(1)}, bf16[2,128,512]{2,1,0:T(8,128)(2,1)S(1)}, u32[]{:S(2)}, u32[]{:S(2)}) collective-permute-start(bf16[2,128,512]{2,1,0:T(8,128)(2,1)S(1)} %bitcast.37), channel_id=1, source_target_pairs={{0,3},{1,0},{2,1},{3,2},{4,7},{5,4},{6,5},{7,6},{8,11},{9,8},{10,9... | collective-permute-start | bytes 786440 | tf_op jit(solution)/shard_map/ppermute | solution.py:500
  10.2 22.4 %copy-start.19 = (bf16[512,2,128]{2,1,0:T(2,128)(2,1)S(1)}, bf16[512,2,128]{2,1,0:T(2,128)(2,1)}, u32[]{:S(2)}) copy-start(bf16[512,2,128]{2,1,0:T(2,128)(2,1)} %param.22) | copy-start | bytes 786436
  10.5 14.6 %copy-start.4 = (f32[4,32,512]{2,1,0:T(8,128)}, f32[4,32,512]{2,1,0:T(8,128)S(1)}, u32[]{:S(2)}) copy-start(f32[4,32,512]{2,1,0:T(8,128)S(1)} %prep.1.prep_ref) | copy-start | bytes 786436
  10.5 27.0 %copy-start.23 = (f32[32]{0:T(128)S(1)}, f32[32]{0:T(128)}, u32[]{:S(2)}) copy-start(f32[32]{0:T(128)} %param.24) | copy-start | bytes 388
  11.2 13.9 %copy-start.12 = (s32[32]{0:T(128)}, s32[32]{0:T(128)S(1)}, u32[]{:S(2)}) copy-start(s32[32]{0:T(128)S(1)} %fusion.slot_ref) | copy-start | bytes 388
  11.6 13.5 %copy-start.7 = (bf16[2,128,512]{2,1,0:T(8,128)(2,1)}, bf16[2,128,512]{2,1,0:T(8,128)(2,1)S(1)}, u32[]{:S(2)}) copy-start(bf16[2,128,512]{2,1,0:T(8,128)(2,1)S(1)} %collective-permute-done.2.i3.m3) | copy-start | bytes 786436
  18.4 6.7 %copy-start.8 = (bf16[2,128,512]{2,1,0:T(8,128)(2,1)}, bf16[2,128,512]{2,1,0:T(8,128)(2,1)S(1)}, u32[]{:S(2)}) copy-start(bf16[2,128,512]{2,1,0:T(8,128)(2,1)S(1)} %collective-permute-done.1.i2.m2) | copy-start | bytes 786436
  18.4 1.7 copy-start.2
  20.1 5.0 %copy-start.9 = (bf16[2,128,512]{2,1,0:T(8,128)(2,1)}, bf16[2,128,512]{2,1,0:T(8,128)(2,1)S(1)}, u32[]{:S(2)}) copy-start(bf16[2,128,512]{2,1,0:T(8,128)(2,1)S(1)} %collective-permute-done.i1.m1) | copy-start | bytes 786436
  25.1 34.5 %collective-permute-start.6 = (bf16[2048,1024]{1,0:T(8,128)(2,1)}, bf16[2048,1024]{1,0:T(8,128)(2,1)}, u32[]{:S(2)}, u32[]{:S(2)}) collective-permute-start(bf16[2048,1024]{1,0:T(8,128)(2,1)} %bitcast.56), channel_id=1, source_target_pairs={{0,4},{4,0},{8,12},{12,8},{16,20},{20,16},{24,28},{28,24},{32,36},... | collective-permute-start | bytes 12582920 | tf_op jit(solution)/shard_map/ppermute | solution.py:552
  25.2 19.3 %all-to-all-start = ((bf16[32,72,128]{2,1,0:T(8,128)(2,1)}), bf16[32,72,128]{2,1,0:T(8,128)(2,1)S(1)}, u32[]{:S(2)}, u32[]{:S(2)}) async-start(bf16[32,72,128]{2,1,0:T(8,128)(2,1)} %get-tuple-element.22), calls=%async_computation | async-start | bytes 1179648 | tf_op jit(solution)/shard_map/all_to_all | solution.py:556
  32.7 17.2 %copy-start.21 = (bf16[512,2,128]{2,0,1:T(8,128)(2,1)}, bf16[512,2,128]{2,0,1:T(8,128)(2,1)S(1)}, u32[]{:S(2)}) copy-start(bf16[512,2,128]{2,0,1:T(8,128)(2,1)S(1)} %copy.32) | copy-start | bytes 786436
  32.7 16.8 %collective-permute-start.5 = (bf16[2,512,128]{2,1,0:T(8,128)(2,1)S(1)}, bf16[2,512,128]{2,1,0:T(8,128)(2,1)S(1)}, u32[]{:S(2)}, u32[]{:S(2)}) collective-permute-start(bf16[2,512,128]{2,1,0:T(8,128)(2,1)S(1)} %bitcast.50), channel_id=1, source_target_pairs={{0,1},{1,2},{2,3},{3,0},{4,5},{5,6},{6,7},{7,4},{8,9},{9,10},{10,1... | collective-permute-start | bytes 786440 | tf_op jit(solution)/shard_map/ppermute | solution.py:500
  33.9 16.0 %collective-permute-start.4 = (bf16[2,512,128]{2,1,0:T(8,128)(2,1)S(1)}, bf16[2,512,128]{2,1,0:T(8,128)(2,1)S(1)}, u32[]{:S(2)}, u32[]{:S(2)}) collective-permute-start(bf16[2,512,128]{2,1,0:T(8,128)(2,1)S(1)} %bitcast.51), channel_id=1, source_target_pairs={{0,2},{1,3},{2,0},{3,1},{4,6},{5,7},{6,4},{7,5},{8,10},{9,11},{10,... | collective-permute-start | bytes 786440 | tf_op jit(solution)/shard_map/ppermute | solution.py:499
  36.3 13.6 %collective-permute-start.3 = (bf16[2,512,128]{2,1,0:T(8,128)(2,1)S(1)}, bf16[2,512,128]{2,1,0:T(8,128)(2,1)S(1)}, u32[]{:S(2)}, u32[]{:S(2)}) collective-permute-start(bf16[2,512,128]{2,1,0:T(8,128)(2,1)S(1)} %bitcast.52), channel_id=1, source_target_pairs={{0,3},{1,0},{2,1},{3,2},{4,7},{5,4},{6,5},{7,6},{8,11},{9,8},{10,9... | collective-permute-start | bytes 786440 | tf_op jit(solution)/shard_map/ppermute | solution.py:500
  37.5 108.9 %collective-permute-start.10 = (bf16[2048,1024]{1,0:T(8,128)(2,1)}, bf16[2048,1024]{1,0:T(8,128)(2,1)}, u32[]{:S(2)}, u32[]{:S(2)}) collective-permute-start(bf16[2048,1024]{1,0:T(8,128)(2,1)} %bitcast.59), channel_id=1, source_target_pairs={{0,4},{4,0},{8,12},{12,8},{16,20},{20,16},{24,28},{28,24},{32,36},... | collective-permute-start | bytes 12582920 | tf_op jit(solution)/shard_map/ppermute | solution.py:553
  45.3 15.3 %all-to-all-start.1 = ((bf16[32,64,128]{2,1,0:T(8,128)(2,1)}), bf16[32,64,128]{2,1,0:T(8,128)(2,1)S(1)}, u32[]{:S(2)}, u32[]{:S(2)}) async-start(bf16[32,64,128]{2,1,0:T(8,128)(2,1)} %scan.1), calls=%async_computation.1 | async-start | bytes 1048576 | tf_op jit(solution)/shard_map/all_to_all | solution.py:563
  49.5 96.9 %collective-permute-start.11 = (bf16[1024,2048]{1,0:T(8,128)(2,1)}, bf16[1024,2048]{1,0:T(8,128)(2,1)}, u32[]{:S(2)}, u32[]{:S(2)}) collective-permute-start(bf16[1024,2048]{1,0:T(8,128)(2,1)} %bitcast.62), channel_id=1, source_target_pairs={{0,4},{4,0},{8,12},{12,8},{16,20},{20,16},{24,28},{28,24},{32,36},... | collective-permute-start | bytes 12582920 | tf_op jit(solution)/shard_map/ppermute | solution.py:554
  61.5 17.2 %copy-start.22 = (s32[128,4]{0,1:T(4,128)S(1)}, s32[128,4]{0,1:T(4,128)}, u32[]{:S(2)}) copy-start(s32[128,4]{0,1:T(4,128)} %param.30) | copy-start | bytes 6148
  61.5 17.3 %copy-start.20 = (bf16[2048,64]{0,1:T(8,128)(2,1)S(1)}, bf16[2048,64]{0,1:T(8,128)(2,1)}, u32[]{:S(2)}) copy-start(bf16[2048,64]{0,1:T(8,128)(2,1)} %param.29) | copy-start | bytes 786436
  61.5 40.3 %copy-start.13 = (bf16[128,2048]{1,0:T(8,128)(2,1)S(1)}, bf16[128,2048]{1,0:T(8,128)(2,1)}, u32[]{:S(2)}) copy-start(bf16[128,2048]{1,0:T(8,128)(2,1)} %residual_ref.1) | copy-start | bytes 1572868
  61.5 40.3 %copy-start.15 = (f32[2048]{0:T(1024)S(1)}, f32[2048]{0:T(1024)}, u32[]{:S(2)}) copy-start(f32[2048]{0:T(1024)} %param.28) | copy-start | bytes 24580
  74.3 16.0 %collective-permute-start.7 = (bf16[128,2048]{1,0:T(8,128)(2,1)}, bf16[128,2048]{1,0:T(8,128)(2,1)S(1)}, u32[]{:S(2)}, u32[]{:S(2)}) collective-permute-start(bf16[128,2048]{1,0:T(8,128)(2,1)} %get-tuple-element.25), channel_id=1, source_target_pairs={{0,1},{1,2},{2,3},{3,0},{4,5},{5,6},{6,7},{7,4},{8,9},{9,10},{10,1... | collective-permute-start | bytes 1572872 | tf_op jit(solution)/shard_map/ppermute | solution.py:609
  75.4 25.5 %collective-permute-start.8 = (bf16[128,2048]{1,0:T(8,128)(2,1)}, bf16[128,2048]{1,0:T(8,128)(2,1)S(1)}, u32[]{:S(2)}, u32[]{:S(2)}) collective-permute-start(bf16[128,2048]{1,0:T(8,128)(2,1)} %get-tuple-element.26), channel_id=1, source_target_pairs={{0,3},{1,0},{2,1},{3,2},{4,7},{5,4},{6,5},{7,6},{8,11},{9,8},{10,9... | collective-permute-start | bytes 1572872 | tf_op jit(solution)/shard_map/ppermute | solution.py:610
  77.5 24.2 %collective-permute-start.9 = (bf16[128,2048]{1,0:T(8,128)(2,1)}, bf16[128,2048]{1,0:T(8,128)(2,1)S(1)}, u32[]{:S(2)}, u32[]{:S(2)}) collective-permute-start(bf16[128,2048]{1,0:T(8,128)(2,1)} %get-tuple-element.27), channel_id=1, source_target_pairs={{0,2},{1,3},{2,0},{3,1},{4,6},{5,7},{6,4},{7,5},{8,10},{9,11},{10,... | collective-permute-start | bytes 1572872 | tf_op jit(solution)/shard_map/ppermute | solution.py:611
  106.7 34.2 %copy-start.5 = (f32[128,2048]{1,0:T(8,128)}, f32[128,2048]{1,0:T(8,128)S(1)}, u32[]{:S(2)}) copy-start(f32[128,2048]{1,0:T(8,128)S(1)} %get-tuple-element.28.base_ref) | copy-start | bytes 3145732
  140.9 31.2 %all-to-all-start.4 = ((bf16[448,8,256]{2,1,0:T(8,128)(2,1)}), bf16[448,8,256]{2,1,0:T(8,128)(2,1)S(1)}, u32[]{:S(2)}, u32[]{:S(2)}) async-start(bf16[448,8,256]{2,1,0:T(8,128)(2,1)} %bitcast.20), calls=%async_computation.4 | async-start | bytes 3670016 | tf_op jit(solution)/shard_map/all_to_all | solution.py:640
  173.4 40.2 %all-to-all-start.3 = ((bf16[448,8,256]{2,1,0:T(8,128)(2,1)}), bf16[448,8,256]{2,1,0:T(8,128)(2,1)S(1)}, u32[]{:S(2)}, u32[]{:S(2)}) async-start(bf16[448,8,256]{2,1,0:T(8,128)(2,1)} %bitcast.45), calls=%async_computation.3 | async-start | bytes 3670016 | tf_op jit(solution)/shard_map/all_to_all | solution.py:640
  214.8 31.4 %all-to-all-start.5 = ((bf16[448,8,256]{2,1,0:T(8,128)(2,1)}), bf16[448,8,256]{2,1,0:T(8,128)(2,1)S(1)}, u32[]{:S(2)}, u32[]{:S(2)}) async-start(bf16[448,8,256]{2,1,0:T(8,128)(2,1)} %bitcast.44), calls=%async_computation.5 | async-start | bytes 3670016 | tf_op jit(solution)/shard_map/all_to_all | solution.py:640
  (12 other events, 11.7 us)
